TPU v7x, 1024 devices: a whole 4x8x16 slice. The times are simulated.
1024 devices in a mesh: replica: 16 (over x_hi, y), fsdp: 16 (over z), tensor: 4 (over x_lo, core).
Axes of the slice: x: 4 (x_hi: 2, x_lo: 2; x = x_hi * 2 + x_lo), y: 8, z: 16, core: 2. Of those that a mesh axis runs over, the one named last changes fastest.
Arguments:
- acts: bfloat16 [16, 4096, 8192], P('replica', 'fsdp', 'tensor'), may hold values from -6 to 6
- key_weight: bfloat16 [16, 512, 8192], P('replica', 'fsdp', 'tensor'), may hold values from -0.0625 to 0.0625
- key_cotangent: bfloat16 [16, 4096, 512], P('replica', 'fsdp', 'tensor'), may hold values from -1.1953125 to 1.1953125
- first_moment: float32 [16, 512, 8192], P('replica', 'fsdp', 'tensor'), may hold values from -3 to 3
- second_moment: float32 [16, 512, 8192], P('replica', 'fsdp', 'tensor'), may hold values from 0.01 to 1
- local_params: bfloat16 [16, 131072, 128], P('replica', ('fsdp', 'tensor')), may hold values from -6 to 6
- outer_params: float32 [16384, 128], P(('fsdp', 'tensor')), may hold values from -6 to 6
- outer_momentum: float32 [16384, 128], P(('fsdp', 'tensor')), may hold values from -3 to 3
- fragment_index: int32 [1], replicated, may hold values from 0 to 7
- slice_offsets: int32 [8], replicated, may hold values from 0 to 1792, as said below
Outputs:
- keys: bfloat16 [16, 4096, 512], P('replica', 'fsdp', 'tensor')
- new_weight: bfloat16 [16, 512, 8192], P('replica', 'fsdp', 'tensor')
- new_first: float32 [16, 512, 8192], P('replica', 'fsdp', 'tensor')
- new_second: float32 [16, 512, 8192], P('replica', 'fsdp', 'tensor')
- synced_params: float32 [16384, 128], P(('fsdp', 'tensor'))
- synced_momentum: float32 [16384, 128], P(('fsdp', 'tensor'))
Inputs may be any that keep to these rules, and one draw needn't show every extreme that they name: `slice_offsets`: distinct multiples of 256, one for each fragment.
All inputs are finite; a program needn't handle non-finite values.
Results may differ from a plain program's by a relative error of at most 0.001.
Values may be sent and summed in bfloat16 or wider, within the bound.
A program may use at most 32 MiB of HBM per device.

v0:
```python
import jax
import jax.numpy as jnp
from jax import lax
from jax.sharding import PartitionSpec as P

beta_first = 0.9
beta_second = 0.95
adam_rate = 0.001
adam_eps = 1e-08
decay_coef = 0.1
outer_rate = 0.7
momentum_coef = 0.9


def on_device(
    acts,
    key_weight,
    key_cotangent,
    first_moment,
    second_moment,
    local_params,
    outer_params,
    outer_momentum,
    fragment_index,
    slice_offsets,
):
    tokens_here = acts[0]
    weight_here = key_weight[0]
    partial_keys = lax.dot_general(
        tokens_here,
        lax.all_gather(weight_here, "fsdp", axis=0, tiled=True),
        (((1,), (1,)), ((), ())),
        preferred_element_type=jnp.float32,
    )
    keys_here = lax.psum_scatter(partial_keys, "tensor", scatter_dimension=1, tiled=True).astype(
        jnp.bfloat16
    )
    cotangent = lax.all_gather(key_cotangent[0], "tensor", axis=1, tiled=True)
    gradient = lax.psum_scatter(
        lax.dot_general(
            cotangent, tokens_here, (((0,), (0,)), ((), ())), preferred_element_type=jnp.float32
        ),
        "fsdp",
        scatter_dimension=0,
        tiled=True,
    )
    first_next = beta_first * first_moment[0] + (1.0 - beta_first) * gradient
    second_next = beta_second * second_moment[0] + (1.0 - beta_second) * gradient * gradient
    weight_float = weight_here.astype(jnp.float32)
    weight_next = weight_float - adam_rate * (
        first_next / (jnp.sqrt(second_next) + adam_eps) + decay_coef * weight_float
    )
    keys = keys_here[None]
    new_weight = weight_next.astype(jnp.bfloat16)[None]
    new_first = first_next[None]
    new_second = second_next[None]
    offset = slice_offsets[fragment_index[0]]
    local_slice = lax.dynamic_slice_in_dim(
        local_params[0], offset, outer_params.shape[0], 0
    ).astype(jnp.float32)
    difference = outer_params - local_slice
    workers = lax.axis_size("replica")
    mean_delta = lax.psum(difference, "replica") / workers
    moment_next = momentum_coef * outer_momentum + mean_delta
    params_next = outer_params - outer_rate * (mean_delta + momentum_coef * moment_next)
    return (keys, new_weight, new_first, new_second, params_next, moment_next)


def solution(mesh):
    in_specs = (
        P("replica", "fsdp", "tensor"),
        P("replica", "fsdp", "tensor"),
        P("replica", "fsdp", "tensor"),
        P("replica", "fsdp", "tensor"),
        P("replica", "fsdp", "tensor"),
        P("replica", ("fsdp", "tensor"), None),
        P(("fsdp", "tensor"), None),
        P(("fsdp", "tensor"), None),
        P(),
        P(),
    )
    out_specs = (
        P("replica", "fsdp", "tensor"),
        P("replica", "fsdp", "tensor"),
        P("replica", "fsdp", "tensor"),
        P("replica", "fsdp", "tensor"),
        P(("fsdp", "tensor"), None),
        P(("fsdp", "tensor"), None),
    )
    return jax.shard_map(
        on_device, mesh=mesh, in_specs=in_specs, out_specs=out_specs, check_vma=False
    )
```

profile of v0, /device:TPU:6, one launch (start us, length us, event | category | flops | bytes accessed | tf_op | source)
XLA Modules:
  0.0 222.1 jit_solution(16894224410186911134)
XLA Ops:
  8.0 0.0 copy-start
  8.0 0.0 all-gather.4.cloned.1.call-start
  8.1 0.7 all-gather.4.cloned.1.call-update
  8.7 0.0 all-reduce.2.cloned.1.call-start
  9.4 1.2 dynamic_slice.6
  12.6 1.6 convert_subtract_fusion.1
  14.3 0.0 all-reduce.2.cloned.1.call-update
  14.3 0.0 copy-start.6
  14.3 0.0 reduce-scatter.3.cloned.1.call-start
  14.3 82.0 %all-gather.4.cloned.1.call-done = bf16[1,512,2048]{2,1,0:T(8,128)(2,1)} async-done(((bf16[1,32,2048]{2,1,0:T(8,128)(2,1)}), bf16[1,512,2048]{2,1,0:T(8,128)(2,1)}) %all-gather.4.cloned.1.call-update) | async-done | bytes 2097168 | tf_op jit(solution)/shard_map/all_gather | solution.py:31
  96.4 0.0 copy-done
  96.4 3.1 %fusion = f32[256,512]{1,0:T(8,128)} fusion(bf16[1,512,2048]{2,1,0:T(8,128)(2,1)} %all-gather.4.cloned.1.call-done, bf16[1,256,2048]{2,1,0:T(8,128)(2,1)S(1)} %copy-done), kind=kOutput, calls=%fused_computation | convolution fusion | flops 536870912 | bytes 3670016 | tf_op jit(solution)/shard_map/dot_general | solution.py:29
  99.5 0.0 reduce-scatter.3.cloned.1.call-update
  99.5 0.0 reduce-scatter.5.cloned.1.call-start
  99.6 0.0 copy-done.6
  99.6 5.8 %all-gather.1 = bf16[1,256,512]{2,1,0:T(8,128)(2,1)S(1)} all-gather(bf16[1,256,128]{2,1,0:T(8,128)(2,1)S(1)} %copy-done.6), channel_id=3, replica_groups=mesh['replica'=16,'fsdp'=16,'tensor'=4] {'tensor'}, dimensions={2}, use_global_device_ids=true | all-gather | bytes 327680 | tf_op jit(solution)/shard_map/all_gather | solution.py:38
  105.4 2.7 %fusion.2 = f32[512,2048]{1,0:T(8,128)} fusion(bf16[1,256,2048]{2,1,0:T(8,128)(2,1)S(1)} %copy-done, bf16[1,256,512]{2,1,0:T(8,128)(2,1)S(1)} %all-gather.1), kind=kOutput, calls=%fused_computation.2 | convolution fusion | flops 536870912 | bytes 5505024 | tf_op jit(solution)/shard_map/dot_general | solution.py:40
  108.1 0.0 copy-start.1
  108.1 0.0 copy-start.5
  108.1 0.0 copy-start.2
  108.1 0.0 copy-start.3
  108.1 0.0 copy-start.4
  108.1 0.0 reduce-scatter.5.cloned.1.call-update
  108.1 82.7 %all-reduce.2.cloned.1.call-done = f32[256,128]{1,0:T(8,128)} async-done(((f32[256,128]{1,0:T(8,128)}), f32[256,128]{1,0:T(8,128)}) %all-reduce.2.cloned.1.call-update) | async-done | bytes 131088 | tf_op jit(solution)/shard_map/psum | solution.py:63
  190.9 0.0 copy-done.1
  190.9 0.0 copy-done.5
  190.9 1.6 multiply_subtract_fusion
  192.5 0.0 reduce-scatter.3.cloned.1.call-done
  192.5 1.5 convert_bitcast_fusion
  194.1 19.0 %reduce-scatter.5.cloned.1.call-done = f32[32,2048]{1,0:T(8,128)} async-done(((f32[512,2048]{1,0:T(8,128)}), f32[32,2048]{1,0:T(8,128)}) %reduce-scatter.5.cloned.1.call-update) | async-done | bytes 262160 | tf_op jit(solution)/shard_map/reduce_scatter | solution.py:39
  213.0 0.0 copy-done.2
  213.0 0.0 copy-done.3
  213.0 0.0 copy-done.4
  213.0 2.0 fusion.12
Async XLA Ops:
  8.0 88.4 %copy-start = (bf16[1,256,2048]{2,1,0:T(8,128)(2,1)S(1)}, bf16[1,256,2048]{2,1,0:T(8,128)(2,1)}, u32[]{:S(2)}) copy-start(bf16[1,256,2048]{2,1,0:T(8,128)(2,1)} %param.10) | copy-start | bytes 3145732
  8.0 88.4 %all-gather.4.cloned.1.call-start = ((), (), s32[]{:S(2)}) async-start(), calls=%async_computation.5 | async-start | bytes 2228224 | tf_op jit(solution)/shard_map/all_gather | solution.py:31
  8.7 182.1 %all-reduce.2.cloned.1.call-start = ((), (), s32[]{:S(2)}) async-start(), calls=%async_computation.4 | async-start | bytes 262144 | tf_op jit(solution)/shard_map/psum | solution.py:63
  14.3 85.3 %copy-start.6 = (bf16[1,256,128]{2,1,0:T(8,128)(2,1)S(1)}, bf16[1,256,128]{2,1,0:T(8,128)(2,1)}, u32[]{:S(2)}) copy-start(bf16[1,256,128]{2,1,0:T(8,128)(2,1)} %param.12) | copy-start | bytes 196612
  14.3 178.2 %reduce-scatter.3.cloned.1.call-start = ((), (), s32[]{:S(2)}) async-start(), calls=%async_computation.2 | async-start | bytes 655360 | tf_op jit(solution)/shard_map/reduce_scatter | solution.py:35
  99.5 113.5 %reduce-scatter.5.cloned.1.call-start = ((), (), s32[]{:S(2)}) async-start(), calls=%async_computation.3 | async-start | bytes 4456448 | tf_op jit(solution)/shard_map/reduce_scatter | solution.py:39
  108.1 82.8 %copy-start.1 = (f32[256,128]{1,0:T(8,128)S(1)}, f32[256,128]{1,0:T(8,128)}, u32[]{:S(2)}) copy-start(f32[256,128]{1,0:T(8,128)} %param.16) | copy-start | bytes 393220
  108.1 82.8 %copy-start.5 = (f32[256,128]{1,0:T(8,128)S(1)}, f32[256,128]{1,0:T(8,128)}, u32[]{:S(2)}) copy-start(f32[256,128]{1,0:T(8,128)} %param.17) | copy-start | bytes 393220
  108.1 104.9 %copy-start.2 = (bf16[1,32,2048]{2,1,0:T(8,128)(2,1)S(1)}, bf16[1,32,2048]{2,1,0:T(8,128)(2,1)}, u32[]{:S(2)}) copy-start(bf16[1,32,2048]{2,1,0:T(8,128)(2,1)} %param.11) | copy-start | bytes 393220
  108.1 104.9 %copy-start.3 = (f32[1,32,2048]{2,1,0:T(8,128)S(1)}, f32[1,32,2048]{2,1,0:T(8,128)}, u32[]{:S(2)}) copy-start(f32[1,32,2048]{2,1,0:T(8,128)} %param.14) | copy-start | bytes 786436
  108.1 104.9 %copy-start.4 = (f32[1,32,2048]{2,1,0:T(8,128)S(1)}, f32[1,32,2048]{2,1,0:T(8,128)}, u32[]{:S(2)}) copy-start(f32[1,32,2048]{2,1,0:T(8,128)} %param.13) | copy-start | bytes 786436
Sparse Core Ops, SparseCore 0:
  11.5 84.8 all-gather.3
  99.8 23.8 reduce-scatter.2
  127.1 85.8 reduce-scatter.4
Sparse Core Ops, SparseCore 1:
  14.4 176.5 all-reduce.1
where the time goes:
time: 223 us; the launch traced here: 222 us
  waiting for transfers between devices  184 us (83%)
  between operations  17.8 us (8%)
  other arithmetic  6.78 us (3%)
  matrix products  5.82 us (3%)
  blocking collectives  5.81 us (3%)
    psum x1, waiting for transfers between devices, on_device(): mean_delta = lax.psum(difference, 'replica') / workers  82.7 us
    all_gather x1, waiting for transfers between devices, on_device(): lax.all_gather(weight_here, 'fsdp', axis=0, tiled=True)  82 us
    reduce_scatter x1, waiting for transfers between devices, on_device(): lax.psum_scatter(lax.dot_general(cotangent, tokens_here, (((0,), (0,)), (...  19 us
    all_gather x1, blocking collectives, on_device(): cotangent = lax.all_gather(key_cotangent[0], 'tensor', axis=1, tiled=True)  5.81 us
  transfers between devices with their start and end apart: 4, of which 3 were waited for; matrix products, arithmetic and copies ran while one was open for 5% of the time, Pallas kernels for 0%

commit v1 on v0

v1 whole, which is shorter than its diff:
```python
import functools

import jax
import jax.numpy as jnp
from jax import lax
from jax.experimental import pallas as pl
from jax.experimental.pallas import tpu as pltpu
from jax.sharding import PartitionSpec as P

MESH = pl.DeviceIdType.MESH
F32 = jnp.float32
LAG = 5
TOP = 32700.0
STEPS = 4.0

beta_first = 0.9
beta_second = 0.95
adam_rate = 0.001
adam_eps = 1e-08
decay_coef = 0.1
outer_rate = 0.7
momentum_coef = 0.9


def kernel(
    n, T, R,
    acts_h, w_h, cot_h, m1_h, m2_h, loc_h, outer_h, mom_h, frag_s, offs_s,
    keys_o, nw_o, nf_o, ns_o, sp_o, sm_o,
    acts_v, w_v, cot_v, g_v, m1_v, m2_v, nw_v, kp_v, kr_v, k_v,
    loc_v, ls_v, outer_v, mom_v, ob_v, mean_v, sp_v,
    su_v, sd_v, ru_v, rd_v,
    lsem, osem, ags, agr, rss, rsr, cs, cr, ks, kr, oas, oar, obs, obr,
):
    z = lax.axis_index("fsdp")
    t = lax.axis_index("tensor")
    r = lax.axis_index("replica")
    h = n // 2
    up = lax.rem(z + 1, n)
    down = lax.rem(z + n - 1, n)
    rows = w_h.shape[1]
    half = rows // 2
    width = w_h.shape[2]
    lanes = min(128, width)
    tiles = width // lanes
    kt = kp_v.shape[2]
    per = n // T
    orow = outer_h.shape[0] // R
    msgs = 2 * h - 1

    def at(axis, index):
        return dict(device_id={axis: index}, device_id_type=MESH)

    core = lax.rem(t, 2)
    side = t // 2
    sib = t + 1 - 2 * core
    peers = [sib, lax.rem(t + 2, 4), lax.rem(sib + 2, 4)]

    def load(src, dst, i):
        c = pltpu.make_async_copy(src, dst, lsem.at[i])
        c.start()
        return c

    l_cot = load(cot_h.at[0], cot_v.at[t], 0)
    l_acts = load(acts_h.at[0], acts_v, 1)
    l_loc = load(loc_h.at[0], loc_v, 2)
    l_outer = load(outer_h, outer_v, 3)
    l_w = load(w_h.at[0], w_v.at[z], 4)
    l_mom = load(mom_h, mom_v, 5)
    l_m1 = load(m1_h.at[0], m1_v, 6)
    l_m2 = load(m2_h.at[0], m2_v, 7)

    barrier = pltpu.get_barrier_semaphore()
    for index in (up, down):
        pl.semaphore_signal(barrier, inc=1, **at("fsdp", index))
    for p in peers:
        pl.semaphore_signal(barrier, inc=1, **at("tensor", p))
    for i in range(1, R):
        pl.semaphore_signal(barrier, inc=1, **at("replica", lax.rem(r + i, R)))
    pl.semaphore_wait(barrier, 2 + len(peers) + R - 1)

    def ag(m, way, receiving=False):
        j, sub = m // 2, (m % 2 if way == 0 else 1 - m % 2)
        j = j + (1 if receiving else 0)
        owner = lax.rem(z + n - j, n) if way == 0 else lax.rem(z + j, n)
        cut = pl.ds(sub * half, half)
        src = w_h.at[0, cut] if (m // 2 == 0 and not receiving) else w_v.at[owner, cut]
        return pltpu.make_async_remote_copy(
            src_ref=src,
            dst_ref=w_v.at[owner, cut],
            send_sem=ags.at[way, m],
            recv_sem=agr.at[way, m],
            **at("fsdp", up if way == 0 else down),
        )

    sends = []

    def ag_tick(m):
        for way in (0, 1):
            if m >= 2:
                ag(m - 2, way, True).wait_recv()
            c = ag(m, way)
            c.start()
            sends.append(c)

    def rs_msg(i, way):
        main = 0 if way == 0 else 1
        if i % 2 == 0:
            return i // 2, main
        return (i + 1) // 2, 1 - main

    def rs(i, way):
        s_buf, r_buf = (su_v, ru_v) if way == 0 else (sd_v, rd_v)
        return pltpu.make_async_remote_copy(
            src_ref=s_buf.at[i],
            dst_ref=r_buf.at[i],
            send_sem=rss.at[way, i],
            recv_sem=rsr.at[way, i],
            **at("fsdp", up if way == 0 else down),
        )

    def scale_of(buf, i):
        code = buf[i, :, width:width + lanes].astype(jnp.int32).astype(F32)
        return jnp.exp2(code * (1.0 / STEPS)) * (1.0 / TOP)

    def rs_tick(i):
        for way in (0, 1):
            s, sub = rs_msg(i, way)
            s_buf, r_buf = (su_v, ru_v) if way == 0 else (sd_v, rd_v)
            d = lax.rem(z + n + h - s, n) if way == 0 else lax.rem(z + n - h + s, n)
            got = i >= 2
            if got:
                rs(i - 2, way).wait_recv()
                scale = scale_of(r_buf, i - 2)
            sums, most = [], None
            for c in range(tiles):
                cols = slice(c * lanes, (c + 1) * lanes)
                x = g_v[d, sub * half:(sub + 1) * half, cols]
                if got:
                    x = x + r_buf[i - 2, :, cols].astype(jnp.int32).astype(F32) * scale
                sums.append(x)
                a = jnp.abs(x)
                most = a if most is None else jnp.maximum(most, a)
            most = jnp.max(most, axis=0, keepdims=True)
            code = jnp.ceil(STEPS * jnp.log2(jnp.maximum(most, 1e-30)))
            inv = TOP * jnp.exp2(code * (-1.0 / STEPS))
            for c in range(tiles):
                cols = slice(c * lanes, (c + 1) * lanes)
                s_buf[i, :, cols] = jnp.round(sums[c] * inv).astype(jnp.int32).astype(jnp.int16)
            s_buf[i, :, width:width + lanes] = jnp.broadcast_to(
                code.astype(jnp.int32), (half, lanes)
            ).astype(jnp.int16)
            c = rs(i, way)
            c.start()
            sends.append(c)

    def cot_copy(k, receiving=False):
        slot = peers[k] if receiving else t
        return pltpu.make_async_remote_copy(
            src_ref=cot_v.at[slot] if receiving else cot_h.at[0],
            dst_ref=cot_v.at[slot],
            send_sem=cs.at[k],
            recv_sem=cr.at[k],
            **at("tensor", peers[k]),
        )

    def key_copy(k):
        return pltpu.make_async_remote_copy(
            src_ref=kp_v.at[peers[k]],
            dst_ref=kr_v.at[k],
            send_sem=ks.at[k],
            recv_sem=kr.at[k],
            **at("tensor", peers[k]),
        )

    def start_cot():
        for k in (1, 2, 0):
            c = cot_copy(k)
            c.start()
            sends.append(c)

    def slice_copy(i, receiving=False):
        to = lax.rem(r + i, R)
        slot = lax.rem(r + R - i, R) if receiving else r
        return pltpu.make_async_remote_copy(
            src_ref=ls_v.at[pl.ds(pl.multiple_of(to * orow, orow), orow)],
            dst_ref=ob_v.at[slot],
            send_sem=oas.at[i],
            recv_sem=oar.at[i],
            **at("replica", to),
        )

    def mean_copy(i, receiving=False):
        to = lax.rem(r + i, R)
        slot = lax.rem(r + R - i, R) if receiving else r
        cut = pl.ds(pl.multiple_of(slot * orow, orow), orow)
        return pltpu.make_async_remote_copy(
            src_ref=mean_v.at[cut],
            dst_ref=mean_v.at[cut],
            send_sem=obs.at[i],
            recv_sem=obr.at[i],
            **at("replica", to),
        )

    def outer_send():
        l_loc.wait()
        size = ls_v.shape[0]
        offset = offs_s[0]
        for f in range(1, offs_s.shape[0]):
            offset = jnp.where(frag_s[0] == f, offs_s[f], offset)
        picked = loc_v[:size, :].astype(F32)
        for b in range(1, loc_v.shape[0] // size):
            piece = loc_v[b * size:(b + 1) * size, :].astype(F32)
            picked = jnp.where(offset == b * size, piece, picked)
        ls_v[...] = picked.astype(jnp.bfloat16)
        for i in range(1, R):
            c = slice_copy(i)
            c.start()
            sends.append(c)

    def outer_mean():
        l_outer.wait()
        mine = pl.ds(pl.multiple_of(r * orow, orow), orow)
        base = outer_v[mine]
        total = base - ls_v[mine].astype(F32)
        for i in range(1, R):
            slice_copy(i, True).wait_recv()
            total = total + (base - ob_v[lax.rem(r + R - i, R)].astype(F32))
        mean_v[mine] = total / R
        for i in range(1, R):
            c = mean_copy(i)
            c.start()
            sends.append(c)

    outs = []

    def store(src, dst, i):
        c = pltpu.make_async_copy(src, dst, osem.at[i])
        c.start()
        outs.append(c)

    def outer_step():
        l_mom.wait()
        for i in range(1, R):
            mean_copy(i, True).wait_recv()
        mean = mean_v[...]
        moment = momentum_coef * mom_v[...] + mean
        mom_v[...] = moment
        sp_v[...] = outer_v[...] - outer_rate * (mean + momentum_coef * moment)
        store(mom_v, sm_o, 0)
        store(sp_v, sp_o, 1)

    def gradient():
        l_acts.wait()
        l_cot.wait()
        for k in range(len(peers)):
            cot_copy(k, True).wait_recv()
        cot = jnp.concatenate([cot_v[k] for k in range(T)], axis=1)
        piece = width // 4
        for c in range(4):
            cols = slice(c * piece, (c + 1) * piece)
            g_v[:, :, cols] = lax.dot_general(
                cot, acts_v[:, cols], (((0,), (0,)), ((), ())), preferred_element_type=F32
            ).reshape(n, rows, piece)

    def keys_part(far):
        u = (1 - side) if far else side
        block = w_v[pl.ds(u * 2 * per, 2 * per)].reshape(2 * per * rows, width)
        got = lax.dot_general(
            acts_v[...], block, (((1,), (1,)), ((), ())), preferred_element_type=F32
        )
        kp_v[2 * u] = got[:, :kt]
        kp_v[2 * u + 1] = got[:, kt:]
        for k in ((1, 2) if far else (0,)):
            c = key_copy(k)
            c.start()
            sends.append(c)

    def keys_end():
        for k in range(len(peers)):
            key_copy(k).wait_recv()
        k_v[...] = (((kp_v[t] + kr_v[0]) + kr_v[1]) + kr_v[2]).astype(jnp.bfloat16)
        store(k_v, keys_o.at[0], 2)

    last = msgs + LAG
    for tick in range(last):
        if tick < msgs:
            ag_tick(tick)
        if tick >= LAG:
            rs_tick(tick - LAG)
        if tick == 1:
            start_cot()
        if tick == min(2, msgs - 1):
            outer_send()
        if tick == LAG - 1:
            gradient()
        if tick == LAG + 1:
            outer_mean()
        if tick == msgs - 1:
            l_w.wait()
            for m in (msgs - 2, msgs - 1):
                for way in (0, 1):
                    ag(m, way, True).wait_recv()
            keys_part(True)
        if tick == msgs:
            keys_part(False)
            outer_step()
    keys_end()

    l_m1.wait()
    l_m2.wait()

    def finish(sub):
        iu = msgs - 1 if sub == 0 else msgs - 2
        idn = msgs - 2 if sub == 0 else msgs - 1
        rs(iu, 0).wait_recv()
        rs(idn, 1).wait_recv()
        su, sd = scale_of(ru_v, iu), scale_of(rd_v, idn)
        rr = slice(sub * half, (sub + 1) * half)
        for c in range(tiles):
            cols = slice(c * lanes, (c + 1) * lanes)
            grad = (
                g_v[z, rr, cols]
                + ru_v[iu, :, cols].astype(jnp.int32).astype(F32) * su
                + rd_v[idn, :, cols].astype(jnp.int32).astype(F32) * sd
            )
            first = beta_first * m1_v[rr, cols] + (1.0 - beta_first) * grad
            second = beta_second * m2_v[rr, cols] + (1.0 - beta_second) * grad * grad
            w = w_v[z, rr, cols].astype(F32)
            new = w - adam_rate * (first / (jnp.sqrt(second) + adam_eps) + decay_coef * w)
            nw_v[rr, cols] = new.astype(jnp.bfloat16)
            m1_v[rr, cols] = first
            m2_v[rr, cols] = second
        cut = pl.ds(sub * half, half)
        store(m1_v.at[cut], nf_o.at[0, cut], 3 + 3 * sub)
        store(m2_v.at[cut], ns_o.at[0, cut], 4 + 3 * sub)
        store(nw_v.at[cut], nw_o.at[0, cut], 5 + 3 * sub)

    finish(0)
    finish(1)
    for c in sends:
        c.wait_send()
    for c in outs:
        c.wait()


def solution(mesh):
    n, T, R = mesh.shape["fsdp"], mesh.shape["tensor"], mesh.shape["replica"]

    def on_device(acts, w, cot, m1, m2, loc, outer, mom, frag, offs):
        tok, width = acts.shape[1:]
        rows = w.shape[1]
        half = rows // 2
        kt = cot.shape[2]
        msgs = n - 1
        lanes = min(128, width)
        bf16 = jnp.bfloat16
        orow = outer.shape[0] // R
        any_ = pl.BlockSpec(memory_space=pl.ANY)
        smem = pl.BlockSpec(memory_space=pltpu.SMEM)
        ring = pltpu.VMEM((msgs, half, width + lanes), jnp.int16)
        dma = pltpu.SemaphoreType.DMA
        return pl.pallas_call(
            functools.partial(kernel, n, T, R),
            out_shape=(
                jax.ShapeDtypeStruct((1, tok, kt), bf16),
                jax.ShapeDtypeStruct(w.shape, bf16),
                jax.ShapeDtypeStruct(m1.shape, F32),
                jax.ShapeDtypeStruct(m2.shape, F32),
                jax.ShapeDtypeStruct(outer.shape, F32),
                jax.ShapeDtypeStruct(mom.shape, F32),
            ),
            in_specs=[pl.BlockSpec(memory_space=pltpu.HBM)] * 8 + [smem] * 2,
            out_specs=[any_] * 6,
            scratch_shapes=[
                pltpu.VMEM((tok, width), bf16),
                pltpu.VMEM((n, rows, width), bf16),
                pltpu.VMEM((T, tok, kt), bf16),
                pltpu.VMEM((n, rows, width), F32),
                pltpu.VMEM((rows, width), F32),
                pltpu.VMEM((rows, width), F32),
                pltpu.VMEM((rows, width), bf16),
                pltpu.VMEM((T, tok, kt), F32),
                pltpu.VMEM((T - 1, tok, kt), F32),
                pltpu.VMEM((tok, kt), bf16),
                pltpu.VMEM(loc.shape[1:], bf16),
                pltpu.VMEM(outer.shape, bf16),
                pltpu.VMEM(outer.shape, F32),
                pltpu.VMEM(outer.shape, F32),
                pltpu.VMEM((R, orow, outer.shape[1]), bf16),
                pltpu.VMEM(outer.shape, F32),
                pltpu.VMEM(outer.shape, F32),
                ring, ring, ring, ring,
                dma((8,)),
                dma((9,)),
                dma((2, msgs)),
                dma((2, msgs)),
                dma((2, msgs)),
                dma((2, msgs)),
                dma((T - 1,)),
                dma((T - 1,)),
                dma((T - 1,)),
                dma((T - 1,)),
                dma((R,)),
                dma((R,)),
                dma((R,)),
                dma((R,)),
            ],
            compiler_params=pltpu.CompilerParams(
                collective_id=0, has_side_effects=True, vmem_limit_bytes=60 * 2**20
            ),
        )(acts, w, cot, m1, m2, loc, outer, mom, frag, offs)

    big = P("replica", "fsdp", "tensor")
    flat = P(("fsdp", "tensor"), None)
    return jax.shard_map(
        on_device,
        mesh=mesh,
        in_specs=(big, big, big, big, big, P("replica", ("fsdp", "tensor"), None), flat, flat, P(), P()),
        out_specs=(big, big, big, big, flat, flat),
        check_vma=False,
    )
```

time: 223 us -> 85.9 us (0.39)
  the two profiles are of different devices: /device:TPU:6 before, /device:TPU:8 now
where the time goes in v1:
time: 85.9 us; the launch traced here: 85.6 us
  Pallas kernels  77.6 us (90%)
  local copies, waits for them, and re-layouts  6.73 us (8%)
  between operations  1.3 us (2%)
    pallas_call x1, Pallas kernels, on_device(): pl.pallas_call(functools.partial(kernel, n, T, R), out_shape=(jax.ShapeDt...  77.6 us
    unnamed x14, local copies, waits for them, and re-layouts  6.73 us

profile of v1, /device:TPU:8, one launch (start us, length us, event | category | flops | bytes accessed | tf_op | source)
XLA Modules:
  0.0 85.6 jit_solution(17927237574095921792)
XLA Ops:
  1.3 77.6 %shard_map.145 = (bf16[1,256,128]{2,1,0:T(8,128)(2,1)}, bf16[1,32,2048]{2,1,0:T(8,128)(2,1)}, f32[1,32,2048]{2,1,0:T(8,128)}, f32[1,32,2048]{2,1,0:T(8,128)}, f32[256,128]{1,0:T(8,128)}, /*index=5*/f32[256,128]{1,0:T(8,128)}) custom-call(bf16[1,256,2048]{2,1,0:T(8,128)(2,1)} %acts_h.1, bf16[1,32,2048]{2,1,0:T(8,128)(2,1)} %w_h.1, ...), custom_call_target="tpu_custom_call" | custom-call | tf_op jit(solution)/shard_map/pallas_call | solution.py:362
  78.8 0.0 copy-start.1
  78.9 1.5 %copy.23 = bf16[1,256,128]{2,1,0:T(8,128)(2,1)} copy(bf16[1,256,128]{2,1,0:T(8,128)(2,1)} %get-tuple-element.12) | data formatting | bytes 131072
  80.4 1.6 %copy.24 = bf16[1,32,2048]{2,1,0:T(8,128)(2,1)} copy(bf16[1,32,2048]{2,1,0:T(8,128)(2,1)} %get-tuple-element.13) | data formatting | bytes 262144
  81.9 0.0 copy-done.1
  81.9 0.0 copy-start
  81.9 0.7 copy.25
  82.6 0.3 copy-done
  83.0 0.0 copy-start.3
  83.0 0.7 copy.26
  83.7 0.3 copy-done.3
  84.0 0.0 copy-start.2
  84.0 0.7 copy.27
  84.6 0.3 copy-done.2
  84.9 0.7 copy.28
Async XLA Ops:
  78.8 3.1 %copy-start.1 = (f32[1,32,2048]{2,1,0:T(8,128)S(1)}, f32[1,32,2048]{2,1,0:T(8,128)}, u32[]{:S(2)}) copy-start(f32[1,32,2048]{2,1,0:T(8,128)} %get-tuple-element.14) | copy-start | bytes 786436
  81.9 1.0 %copy-start = (f32[1,32,2048]{2,1,0:T(8,128)S(1)}, f32[1,32,2048]{2,1,0:T(8,128)}, u32[]{:S(2)}) copy-start(f32[1,32,2048]{2,1,0:T(8,128)} %get-tuple-element.15) | copy-start | bytes 786436
  83.0 1.0 %copy-start.3 = (f32[256,128]{1,0:T(8,128)S(1)}, f32[256,128]{1,0:T(8,128)}, u32[]{:S(2)}) copy-start(f32[256,128]{1,0:T(8,128)} %get-tuple-element.16) | copy-start | bytes 393220
  84.0 1.0 %copy-start.2 = (f32[256,128]{1,0:T(8,128)S(1)}, f32[256,128]{1,0:T(8,128)}, u32[]{:S(2)}) copy-start(f32[256,128]{1,0:T(8,128)} %get-tuple-element.17) | copy-start | bytes 393220

commit v2 on v1

--- a/solution.py
+++ b/solution.py
@@ -9,7 +9,9 @@
 
 MESH = pl.DeviceIdType.MESH
 F32 = jnp.float32
-LAG = 5
+LAG = 3
+CA = 1
+CR = 1
 TOP = 32700.0
 STEPS = 4.0
 
@@ -41,7 +43,6 @@
     half = rows // 2
     width = w_h.shape[2]
     lanes = min(128, width)
-    tiles = width // lanes
     kt = kp_v.shape[2]
     per = n // T
     orow = outer_h.shape[0] // R
@@ -78,15 +79,19 @@
         pl.semaphore_signal(barrier, inc=1, **at("replica", lax.rem(r + i, R)))
     pl.semaphore_wait(barrier, 2 + len(peers) + R - 1)
 
+    acut = width // CA
+
     def ag(m, way, receiving=False):
-        j, sub = m // 2, (m % 2 if way == 0 else 1 - m % 2)
-        j = j + (1 if receiving else 0)
-        owner = lax.rem(z + n - j, n) if way == 0 else lax.rem(z + j, n)
-        cut = pl.ds(sub * half, half)
-        src = w_h.at[0, cut] if (m // 2 == 0 and not receiving) else w_v.at[owner, cut]
+        j, q = m // (2 * CA), m % (2 * CA)
+        sub, col = (q // CA if way == 0 else 1 - q // CA), q % CA
+        hop = j + (1 if receiving else 0)
+        owner = lax.rem(z + n - hop, n) if way == 0 else lax.rem(z + hop, n)
+        cut, cols = pl.ds(sub * half, half), pl.ds(col * acut, acut)
+        own = j == 0 and not receiving
+        src = w_h.at[0, cut, cols] if own else w_v.at[owner, cut, cols]
         return pltpu.make_async_remote_copy(
             src_ref=src,
-            dst_ref=w_v.at[owner, cut],
+            dst_ref=w_v.at[owner, cut, cols],
             send_sem=ags.at[way, m],
             recv_sem=agr.at[way, m],
             **at("fsdp", up if way == 0 else down),
@@ -96,17 +101,22 @@
 
     def ag_tick(m):
         for way in (0, 1):
-            if m >= 2:
-                ag(m - 2, way, True).wait_recv()
+            if m >= 2 * CA:
+                ag(m - 2 * CA, way, True).wait_recv()
             c = ag(m, way)
             c.start()
             sends.append(c)
+
+    rcut = width // CR
+    rtiles = rcut // lanes
 
     def rs_msg(i, way):
         main = 0 if way == 0 else 1
-        if i % 2 == 0:
-            return i // 2, main
-        return (i + 1) // 2, 1 - main
+        if i < CR:
+            return 0, main, i
+        k = i - CR
+        q = k % (2 * CR)
+        return 1 + k // (2 * CR), (1 - main if q < CR else main), q % CR
 
     def rs(i, way):
         s_buf, r_buf = (su_v, ru_v) if way == 0 else (sd_v, rd_v)
@@ -119,34 +129,35 @@
         )
 
     def scale_of(buf, i):
-        code = buf[i, :, width:width + lanes].astype(jnp.int32).astype(F32)
+        code = buf[i, :, rcut:rcut + lanes].astype(jnp.int32).astype(F32)
         return jnp.exp2(code * (1.0 / STEPS)) * (1.0 / TOP)
 
     def rs_tick(i):
         for way in (0, 1):
-            s, sub = rs_msg(i, way)
+            s, sub, col = rs_msg(i, way)
             s_buf, r_buf = (su_v, ru_v) if way == 0 else (sd_v, rd_v)
             d = lax.rem(z + n + h - s, n) if way == 0 else lax.rem(z + n - h + s, n)
-            got = i >= 2
-            if got:
-                rs(i - 2, way).wait_recv()
-                scale = scale_of(r_buf, i - 2)
+            last = i - 2 * CR
+            if last >= 0:
+                rs(last, way).wait_recv()
+                scale = scale_of(r_buf, last)
             sums, most = [], None
-            for c in range(tiles):
-                cols = slice(c * lanes, (c + 1) * lanes)
-                x = g_v[d, sub * half:(sub + 1) * half, cols]
-                if got:
-                    x = x + r_buf[i - 2, :, cols].astype(jnp.int32).astype(F32) * scale
+            for c in range(rtiles):
+                here = slice(c * lanes, (c + 1) * lanes)
+                whole = slice(col * rcut + c * lanes, col * rcut + (c + 1) * lanes)
+                x = g_v[d, sub * half:(sub + 1) * half, whole]
+                if last >= 0:
+                    x = x + r_buf[last, :, here].astype(jnp.int32).astype(F32) * scale
                 sums.append(x)
                 a = jnp.abs(x)
                 most = a if most is None else jnp.maximum(most, a)
             most = jnp.max(most, axis=0, keepdims=True)
             code = jnp.ceil(STEPS * jnp.log2(jnp.maximum(most, 1e-30)))
             inv = TOP * jnp.exp2(code * (-1.0 / STEPS))
-            for c in range(tiles):
-                cols = slice(c * lanes, (c + 1) * lanes)
-                s_buf[i, :, cols] = jnp.round(sums[c] * inv).astype(jnp.int32).astype(jnp.int16)
-            s_buf[i, :, width:width + lanes] = jnp.broadcast_to(
+            for c in range(rtiles):
+                here = slice(c * lanes, (c + 1) * lanes)
+                s_buf[i, :, here] = jnp.round(sums[c] * inv).astype(jnp.int32).astype(jnp.int16)
+            s_buf[i, :, rcut:rcut + lanes] = jnp.broadcast_to(
                 code.astype(jnp.int32), (half, lanes)
             ).astype(jnp.int16)
             c = rs(i, way)
@@ -281,23 +292,22 @@
         k_v[...] = (((kp_v[t] + kr_v[0]) + kr_v[1]) + kr_v[2]).astype(jnp.bfloat16)
         store(k_v, keys_o.at[0], 2)
 
-    last = msgs + LAG
-    for tick in range(last):
-        if tick < msgs:
-            ag_tick(tick)
-        if tick >= LAG:
-            rs_tick(tick - LAG)
-        if tick == 1:
-            start_cot()
-        if tick == min(2, msgs - 1):
-            outer_send()
+    start_cot()
+    for tick in range(msgs + LAG):
+        for k in range(max(CA, CR)):
+            if tick < msgs and k < CA:
+                ag_tick(tick * CA + k)
+            if tick >= LAG and k < CR:
+                rs_tick((tick - LAG) * CR + k)
         if tick == LAG - 1:
             gradient()
-        if tick == LAG + 1:
+        if tick == min(LAG + 1, msgs - 1):
+            outer_send()
+        if tick == min(LAG + 4, msgs - 1):
             outer_mean()
         if tick == msgs - 1:
             l_w.wait()
-            for m in (msgs - 2, msgs - 1):
+            for m in range((msgs - 2) * CA, msgs * CA):
                 for way in (0, 1):
                     ag(m, way, True).wait_recv()
             keys_part(True)
@@ -309,19 +319,20 @@
     l_m1.wait()
     l_m2.wait()
 
-    def finish(sub):
-        iu = msgs - 1 if sub == 0 else msgs - 2
-        idn = msgs - 2 if sub == 0 else msgs - 1
+    def finish(sub, col):
+        iu = (msgs - 1 if sub == 0 else msgs - 2) * CR + col
+        idn = (msgs - 2 if sub == 0 else msgs - 1) * CR + col
         rs(iu, 0).wait_recv()
         rs(idn, 1).wait_recv()
         su, sd = scale_of(ru_v, iu), scale_of(rd_v, idn)
         rr = slice(sub * half, (sub + 1) * half)
-        for c in range(tiles):
-            cols = slice(c * lanes, (c + 1) * lanes)
+        for c in range(rtiles):
+            here = slice(c * lanes, (c + 1) * lanes)
+            cols = slice(col * rcut + c * lanes, col * rcut + (c + 1) * lanes)
             grad = (
                 g_v[z, rr, cols]
-                + ru_v[iu, :, cols].astype(jnp.int32).astype(F32) * su
-                + rd_v[idn, :, cols].astype(jnp.int32).astype(F32) * sd
+                + ru_v[iu, :, here].astype(jnp.int32).astype(F32) * su
+                + rd_v[idn, :, here].astype(jnp.int32).astype(F32) * sd
             )
             first = beta_first * m1_v[rr, cols] + (1.0 - beta_first) * grad
             second = beta_second * m2_v[rr, cols] + (1.0 - beta_second) * grad * grad
@@ -330,16 +341,28 @@
             nw_v[rr, cols] = new.astype(jnp.bfloat16)
             m1_v[rr, cols] = first
             m2_v[rr, cols] = second
+
+    for sub in (0, 1):
+        for col in range(CR):
+            finish(sub, col)
         cut = pl.ds(sub * half, half)
         store(m1_v.at[cut], nf_o.at[0, cut], 3 + 3 * sub)
         store(m2_v.at[cut], ns_o.at[0, cut], 4 + 3 * sub)
         store(nw_v.at[cut], nw_o.at[0, cut], 5 + 3 * sub)
-
-    finish(0)
-    finish(1)
     for c in sends:
         c.wait_send()
     for c in outs:
+        c.wait()
+
+
+def writer(*refs):
+    k = len(refs) // 2
+    sem = refs[-1]
+    ins, outs = refs[:k], refs[k:2 * k]
+    copies = [pltpu.make_async_copy(a, b, sem.at[i]) for i, (a, b) in enumerate(zip(ins, outs))]
+    for c in copies:
+        c.start()
+    for c in copies:
         c.wait()
 
 
@@ -357,18 +380,26 @@
         orow = outer.shape[0] // R
         any_ = pl.BlockSpec(memory_space=pl.ANY)
         smem = pl.BlockSpec(memory_space=pltpu.SMEM)
-        ring = pltpu.VMEM((msgs, half, width + lanes), jnp.int16)
+        ring = pltpu.VMEM((msgs * CR, half, width // CR + lanes), jnp.int16)
         dma = pltpu.SemaphoreType.DMA
-        return pl.pallas_call(
+        results = tuple(
+            jax.ShapeDtypeStruct(*s)
+            for s in (
+                ((1, tok, kt), bf16),
+                (w.shape, bf16),
+                (m1.shape, F32),
+                (m2.shape, F32),
+                (outer.shape, F32),
+                (mom.shape, F32),
+            )
+        )
+        big_args = [
+            pltpu.with_memory_space_constraint(a, pltpu.HBM)
+            for a in (acts, w, cot, m1, m2, loc, outer, mom)
+        ]
+        held = pl.pallas_call(
             functools.partial(kernel, n, T, R),
-            out_shape=(
-                jax.ShapeDtypeStruct((1, tok, kt), bf16),
-                jax.ShapeDtypeStruct(w.shape, bf16),
-                jax.ShapeDtypeStruct(m1.shape, F32),
-                jax.ShapeDtypeStruct(m2.shape, F32),
-                jax.ShapeDtypeStruct(outer.shape, F32),
-                jax.ShapeDtypeStruct(mom.shape, F32),
-            ),
+            out_shape=results,
             in_specs=[pl.BlockSpec(memory_space=pltpu.HBM)] * 8 + [smem] * 2,
             out_specs=[any_] * 6,
             scratch_shapes=[
@@ -392,10 +423,10 @@
                 ring, ring, ring, ring,
                 dma((8,)),
                 dma((9,)),
-                dma((2, msgs)),
-                dma((2, msgs)),
-                dma((2, msgs)),
-                dma((2, msgs)),
+                dma((2, msgs * CA)),
+                dma((2, msgs * CA)),
+                dma((2, msgs * CR)),
+                dma((2, msgs * CR)),
                 dma((T - 1,)),
                 dma((T - 1,)),
                 dma((T - 1,)),
@@ -406,9 +437,17 @@
                 dma((R,)),
             ],
             compiler_params=pltpu.CompilerParams(
-                collective_id=0, has_side_effects=True, vmem_limit_bytes=60 * 2**20
+                collective_id=0, has_side_effects=True, vmem_limit_bytes=40 * 2**20
             ),
-        )(acts, w, cot, m1, m2, loc, outer, mom, frag, offs)
+        )(*big_args, frag, offs)
+        return pl.pallas_call(
+            writer,
+            out_shape=results,
+            in_specs=[any_] * 6,
+            out_specs=[any_] * 6,
+            scratch_shapes=[dma((6,))],
+            compiler_params=pltpu.CompilerParams(vmem_limit_bytes=16 * 2**20),
+        )(*[pltpu.with_memory_space_constraint(a, pltpu.VMEM) for a in held])
 
     big = P("replica", "fsdp", "tensor")
     flat = P(("fsdp", "tensor"), None)

time: 85.9 us -> 80.6 us (0.938)
  the two profiles are of different devices: /device:TPU:8 before, /device:TPU:1 now
where the time goes in v2:
time: 80.6 us; the launch traced here: 80.4 us
  Pallas kernels  79.1 us (98%)
  between operations  1.32 us (2%)
    pallas_call x1, Pallas kernels, on_device(): pl.pallas_call(functools.partial(kernel, n, T, R), out_shape=results, in_...  78.1 us

profile of v2, /device:TPU:1, one launch (start us, length us, event | category | flops | bytes accessed | tf_op | source)
XLA Modules:
  0.0 80.4 jit_solution(5796372053547481411)
XLA Ops:
  0.6 0.0 copy-start
  1.3 0.0 copy-done
  1.3 78.1 %shard_map.145 = (bf16[1,256,128]{2,1,0:T(8,128)(2,1)S(1)}, bf16[1,32,2048]{2,1,0:T(8,128)(2,1)S(1)}, f32[1,32,2048]{2,1,0:T(8,128)S(1)}, f32[1,32,2048]{2,1,0:T...) custom-call(bf16[1,256,2048]{2,1,0:T(8,128)(2,1)} %acts_h.1, bf16[1,32,2048]{2,1,0:T(8,128)(2,1)} %w_h.1, ...), custom_call_target="tpu_custom_call" | custom-call | tf_op jit(solution)/shard_map/pallas_call | solution.py:400
  79.4 1.0 %shard_map.146 = (bf16[1,256,128]{2,1,0:T(8,128)(2,1)}, bf16[1,32,2048]{2,1,0:T(8,128)(2,1)}, f32[1,32,2048]{2,1,0:T(8,128)}, f32[1,32,2048]{2,1,0:T(8,128)}, f32[256,128]{1,0:T(8,128)}, /*index=5*/f32[256,128]{1,0:T(8,128)}) custom-call(bf16[1,256,128]{2,1,0:T(8,128)(2,1)S(1)} %get-tuple-element.12.refs_0_, ...), custom_call_target="tpu_custom_call" | custom-call | tf_op jit(solution)/shard_map/pallas_call | solution.py:443
Async XLA Ops:
  0.6 0.7 copy-start

commit v3 on v2

--- a/solution.py
+++ b/solution.py
@@ -9,9 +9,9 @@
 
 MESH = pl.DeviceIdType.MESH
 F32 = jnp.float32
-LAG = 3
 CA = 1
 CR = 1
+GRADIENT = 3
 TOP = 32700.0
 STEPS = 4.0
 
@@ -26,11 +26,11 @@
 
 def kernel(
     n, T, R,
-    acts_h, w_h, cot_h, m1_h, m2_h, loc_h, outer_h, mom_h, frag_s, offs_s,
+    acts_h, w_h, cot_h, m1_h, m2_h, loc_h, outer_h, mom_h, frag_s, offs_h,
     keys_o, nw_o, nf_o, ns_o, sp_o, sm_o,
     acts_v, w_v, cot_v, g_v, m1_v, m2_v, nw_v, kp_v, kr_v, k_v,
     loc_v, ls_v, outer_v, mom_v, ob_v, mean_v, sp_v,
-    su_v, sd_v, ru_v, rd_v,
+    su_v, sd_v, ru_v, rd_v, offs_s,
     lsem, osem, ags, agr, rss, rsr, cs, cr, ks, kr, oas, oar, obs, obr,
 ):
     z = lax.axis_index("fsdp")
@@ -61,6 +61,14 @@
         c.start()
         return c
 
+    barrier = pltpu.get_barrier_semaphore()
+    for index in (up, down):
+        pl.semaphore_signal(barrier, inc=1, **at("fsdp", index))
+    for p in peers:
+        pl.semaphore_signal(barrier, inc=1, **at("tensor", p))
+    for i in range(1, R):
+        pl.semaphore_signal(barrier, inc=1, **at("replica", lax.rem(r + i, R)))
+
     l_cot = load(cot_h.at[0], cot_v.at[t], 0)
     l_acts = load(acts_h.at[0], acts_v, 1)
     l_loc = load(loc_h.at[0], loc_v, 2)
@@ -69,14 +77,8 @@
     l_mom = load(mom_h, mom_v, 5)
     l_m1 = load(m1_h.at[0], m1_v, 6)
     l_m2 = load(m2_h.at[0], m2_v, 7)
-
-    barrier = pltpu.get_barrier_semaphore()
-    for index in (up, down):
-        pl.semaphore_signal(barrier, inc=1, **at("fsdp", index))
-    for p in peers:
-        pl.semaphore_signal(barrier, inc=1, **at("tensor", p))
-    for i in range(1, R):
-        pl.semaphore_signal(barrier, inc=1, **at("replica", lax.rem(r + i, R)))
+    l_offs = load(offs_h, offs_s, 8)
+
     pl.semaphore_wait(barrier, 2 + len(peers) + R - 1)
 
     acut = width // CA
@@ -174,13 +176,28 @@
             **at("tensor", peers[k]),
         )
 
-    def key_copy(k):
-        return pltpu.make_async_remote_copy(
-            src_ref=kp_v.at[peers[k]],
-            dst_ref=kr_v.at[k],
-            send_sem=ks.at[k],
-            recv_sem=kr.at[k],
-            **at("tensor", peers[k]),
+    home = z // per
+    turn = jnp.where(lax.rem(z, per) < per // 2, T - 1, 1)
+    blocks = [home, lax.rem(home + turn, T), lax.rem(home + T - turn, T), lax.rem(home + T // 2, T)]
+
+    def key_copy(o):
+        b = blocks[o]
+        slot = lax.rem(t - b + 2 * T - 1, T)
+        return pltpu.make_async_remote_copy(
+            src_ref=kp_v.at[b],
+            dst_ref=kr_v.at[slot],
+            send_sem=ks.at[o],
+            recv_sem=kr.at[slot],
+            **at("tensor", b),
+        )
+
+    def key_arrival(slot):
+        return pltpu.make_async_remote_copy(
+            src_ref=kp_v.at[0],
+            dst_ref=kr_v.at[slot],
+            send_sem=ks.at[0],
+            recv_sem=kr.at[slot],
+            **at("tensor", sib),
         )
 
     def start_cot():
@@ -214,6 +231,7 @@
 
     def outer_send():
         l_loc.wait()
+        l_offs.wait()
         size = ls_v.shape[0]
         offset = offs_s[0]
         for f in range(1, offs_s.shape[0]):
@@ -273,47 +291,63 @@
                 cot, acts_v[:, cols], (((0,), (0,)), ((), ())), preferred_element_type=F32
             ).reshape(n, rows, piece)
 
-    def keys_part(far):
-        u = (1 - side) if far else side
-        block = w_v[pl.ds(u * 2 * per, 2 * per)].reshape(2 * per * rows, width)
-        got = lax.dot_general(
+    def key_block(o):
+        b = blocks[o]
+        block = w_v[pl.ds(b * per, per)].reshape(per * rows, width)
+        kp_v[b] = lax.dot_general(
             acts_v[...], block, (((1,), (1,)), ((), ())), preferred_element_type=F32
         )
-        kp_v[2 * u] = got[:, :kt]
-        kp_v[2 * u + 1] = got[:, kt:]
-        for k in ((1, 2) if far else (0,)):
-            c = key_copy(k)
-            c.start()
-            sends.append(c)
+
+        @pl.when(t != b)
+        def _():
+            key_copy(o).start()
 
     def keys_end():
-        for k in range(len(peers)):
-            key_copy(k).wait_recv()
+        for slot in range(T - 1):
+            key_arrival(slot).wait_recv()
         k_v[...] = (((kp_v[t] + kr_v[0]) + kr_v[1]) + kr_v[2]).astype(jnp.bfloat16)
         store(k_v, keys_o.at[0], 2)
 
+    def keys_sent():
+        for o in range(T):
+            @pl.when(t != blocks[o])
+            def _():
+                key_copy(o).wait_send()
+
+    begin = min(GRADIENT, msgs - 1)
+    late = msgs - 1
+    first_keys = (7, 12) if msgs == 15 else (late, late)
     start_cot()
-    for tick in range(msgs + LAG):
-        for k in range(max(CA, CR)):
-            if tick < msgs and k < CA:
-                ag_tick(tick * CA + k)
-            if tick >= LAG and k < CR:
-                rs_tick((tick - LAG) * CR + k)
-        if tick == LAG - 1:
+    l_w.wait()
+    for tick in range(begin + msgs - 1):
+        if tick < msgs:
+            ag_tick(tick)
+        if tick > begin:
+            rs_tick(tick - begin + 1)
+        if tick == begin:
             gradient()
-        if tick == min(LAG + 1, msgs - 1):
+            rs_tick(0)
+            rs_tick(1)
+        if tick == begin + 1:
             outer_send()
-        if tick == min(LAG + 4, msgs - 1):
+        if tick == begin + 4:
             outer_mean()
-        if tick == msgs - 1:
-            l_w.wait()
-            for m in range((msgs - 2) * CA, msgs * CA):
+        if tick == late:
+            for m in range(msgs - 2, msgs):
                 for way in (0, 1):
                     ag(m, way, True).wait_recv()
-            keys_part(True)
-        if tick == msgs:
-            keys_part(False)
+        for o in (0, 1):
+            if tick == first_keys[o]:
+                key_block(o)
+        if tick == late:
+            key_block(2)
+            key_block(3)
+        if tick == begin + 7:
             outer_step()
+    if begin + 4 >= begin + msgs - 1:
+        outer_mean()
+    if begin + 7 >= begin + msgs - 1:
+        outer_step()
     keys_end()
 
     l_m1.wait()
@@ -349,6 +383,7 @@
         store(m1_v.at[cut], nf_o.at[0, cut], 3 + 3 * sub)
         store(m2_v.at[cut], ns_o.at[0, cut], 4 + 3 * sub)
         store(nw_v.at[cut], nw_o.at[0, cut], 5 + 3 * sub)
+    keys_sent()
     for c in sends:
         c.wait_send()
     for c in outs:
@@ -378,8 +413,8 @@
         lanes = min(128, width)
         bf16 = jnp.bfloat16
         orow = outer.shape[0] // R
+        hbm = pl.BlockSpec(memory_space=pltpu.HBM)
         any_ = pl.BlockSpec(memory_space=pl.ANY)
-        smem = pl.BlockSpec(memory_space=pltpu.SMEM)
         ring = pltpu.VMEM((msgs * CR, half, width // CR + lanes), jnp.int16)
         dma = pltpu.SemaphoreType.DMA
         results = tuple(
@@ -400,7 +435,7 @@
         held = pl.pallas_call(
             functools.partial(kernel, n, T, R),
             out_shape=results,
-            in_specs=[pl.BlockSpec(memory_space=pltpu.HBM)] * 8 + [smem] * 2,
+            in_specs=[hbm] * 8 + [pl.BlockSpec(memory_space=pltpu.SMEM), hbm],
             out_specs=[any_] * 6,
             scratch_shapes=[
                 pltpu.VMEM((tok, width), bf16),
@@ -411,7 +446,7 @@
                 pltpu.VMEM((rows, width), F32),
                 pltpu.VMEM((rows, width), bf16),
                 pltpu.VMEM((T, tok, kt), F32),
-                pltpu.VMEM((T - 1, tok, kt), F32),
+                pltpu.VMEM((T, tok, kt), F32),
                 pltpu.VMEM((tok, kt), bf16),
                 pltpu.VMEM(loc.shape[1:], bf16),
                 pltpu.VMEM(outer.shape, bf16),
@@ -421,7 +456,8 @@
                 pltpu.VMEM(outer.shape, F32),
                 pltpu.VMEM(outer.shape, F32),
                 ring, ring, ring, ring,
-                dma((8,)),
+                pltpu.SMEM(offs.shape, jnp.int32),
+                dma((10,)),
                 dma((9,)),
                 dma((2, msgs * CA)),
                 dma((2, msgs * CA)),
@@ -429,8 +465,8 @@
                 dma((2, msgs * CR)),
                 dma((T - 1,)),
                 dma((T - 1,)),
-                dma((T - 1,)),
-                dma((T - 1,)),
+                dma((T,)),
+                dma((T,)),
                 dma((R,)),
                 dma((R,)),
                 dma((R,)),
@@ -439,7 +475,7 @@
             compiler_params=pltpu.CompilerParams(
                 collective_id=0, has_side_effects=True, vmem_limit_bytes=40 * 2**20
             ),
-        )(*big_args, frag, offs)
+        )(*big_args, frag, pltpu.with_memory_space_constraint(offs, pltpu.HBM))
         return pl.pallas_call(
             writer,
             out_shape=results,

time: 80.6 us -> 77.8 us (0.965)
  the two profiles are of different devices: /device:TPU:1 before, /device:TPU:8 now
where the time goes in v3:
time: 77.8 us; the launch traced here: 77.5 us
  Pallas kernels  76.2 us (98%)
  between operations  1.29 us (2%)
    pallas_call x1, Pallas kernels, on_device(): pl.pallas_call(functools.partial(kernel, n, T, R), out_shape=results, in_...  75.2 us

profile of v3, /device:TPU:8, one launch (start us, length us, event | category | flops | bytes accessed | tf_op | source)
XLA Modules:
  0.0 77.5 jit_solution(5137773345022172088)
XLA Ops:
  1.3 75.2 %shard_map.145 = (bf16[1,256,128]{2,1,0:T(8,128)(2,1)S(1)}, bf16[1,32,2048]{2,1,0:T(8,128)(2,1)S(1)}, f32[1,32,2048]{2,1,0:T(8,128)S(1)}, f32[1,32,2048]{2,1,0:T...) custom-call(bf16[1,256,2048]{2,1,0:T(8,128)(2,1)} %acts_h.1, bf16[1,32,2048]{2,1,0:T(8,128)(2,1)} %w_h.1, ...), custom_call_target="tpu_custom_call" | custom-call | tf_op jit(solution)/shard_map/pallas_call | solution.py:435
  76.5 1.0 %shard_map.146 = (bf16[1,256,128]{2,1,0:T(8,128)(2,1)}, bf16[1,32,2048]{2,1,0:T(8,128)(2,1)}, f32[1,32,2048]{2,1,0:T(8,128)}, f32[1,32,2048]{2,1,0:T(8,128)}, f32[256,128]{1,0:T(8,128)}, /*index=5*/f32[256,128]{1,0:T(8,128)}) custom-call(bf16[1,256,128]{2,1,0:T(8,128)(2,1)S(1)} %get-tuple-element.12.refs_0_, ...), custom_call_target="tpu_custom_call" | custom-call | tf_op jit(solution)/shard_map/pallas_call | solution.py:479

commit v4 on v3

--- a/solution.py
+++ b/solution.py
@@ -317,18 +317,18 @@
     begin = min(GRADIENT, msgs - 1)
     late = msgs - 1
     first_keys = (7, 12) if msgs == 15 else (late, late)
-    start_cot()
-    l_w.wait()
     for tick in range(begin + msgs - 1):
         if tick < msgs:
             ag_tick(tick)
+        if tick == 0:
+            start_cot()
         if tick > begin:
             rs_tick(tick - begin + 1)
         if tick == begin:
             gradient()
             rs_tick(0)
             rs_tick(1)
-        if tick == begin + 1:
+        if tick == min(1, late):
             outer_send()
         if tick == begin + 4:
             outer_mean()
@@ -336,11 +336,14 @@
             for m in range(msgs - 2, msgs):
                 for way in (0, 1):
                     ag(m, way, True).wait_recv()
+        if tick == first_keys[0]:
+            l_w.wait()
         for o in (0, 1):
             if tick == first_keys[o]:
                 key_block(o)
         if tick == late:
             key_block(2)
+        if tick == late + 1:
             key_block(3)
         if tick == begin + 7:
             outer_step()
@@ -348,8 +351,6 @@
         outer_mean()
     if begin + 7 >= begin + msgs - 1:
         outer_step()
-    keys_end()
-
     l_m1.wait()
     l_m2.wait()
 
@@ -383,6 +384,7 @@
         store(m1_v.at[cut], nf_o.at[0, cut], 3 + 3 * sub)
         store(m2_v.at[cut], ns_o.at[0, cut], 4 + 3 * sub)
         store(nw_v.at[cut], nw_o.at[0, cut], 5 + 3 * sub)
+    keys_end()
     keys_sent()
     for c in sends:
         c.wait_send()

time: 77.8 us -> 77.2 us (level)
  no operation moved by 1% of the time
where the time goes in v4:
time: 77.2 us; the launch traced here: 77 us
  Pallas kernels  75.7 us (98%)
  between operations  1.29 us (2%)
    pallas_call x1, Pallas kernels, on_device(): pl.pallas_call(functools.partial(kernel, n, T, R), out_shape=results, in_...  74.7 us

profile of v4, /device:TPU:8, one launch (start us, length us, event | category | flops | bytes accessed | tf_op | source)
XLA Modules:
  0.0 77.0 jit_solution(2980788487678193441)
XLA Ops:
  1.3 74.7 %shard_map.145 = (bf16[1,256,128]{2,1,0:T(8,128)(2,1)S(1)}, bf16[1,32,2048]{2,1,0:T(8,128)(2,1)S(1)}, f32[1,32,2048]{2,1,0:T(8,128)S(1)}, f32[1,32,2048]{2,1,0:T...) custom-call(bf16[1,256,2048]{2,1,0:T(8,128)(2,1)} %acts_h.1, bf16[1,32,2048]{2,1,0:T(8,128)(2,1)} %w_h.1, ...), custom_call_target="tpu_custom_call" | custom-call | tf_op jit(solution)/shard_map/pallas_call | solution.py:437
  76.0 1.0 %shard_map.146 = (bf16[1,256,128]{2,1,0:T(8,128)(2,1)}, bf16[1,32,2048]{2,1,0:T(8,128)(2,1)}, f32[1,32,2048]{2,1,0:T(8,128)}, f32[1,32,2048]{2,1,0:T(8,128)}, f32[256,128]{1,0:T(8,128)}, /*index=5*/f32[256,128]{1,0:T(8,128)}) custom-call(bf16[1,256,128]{2,1,0:T(8,128)(2,1)S(1)} %get-tuple-element.12.refs_0_, ...), custom_call_target="tpu_custom_call" | custom-call | tf_op jit(solution)/shard_map/pallas_call | solution.py:481
